TPU v7x, 128 devices: a whole 4x4x4 slice. The times are simulated.
128 devices in a mesh: section: 2 (over y_hi), shard: 16 (over y_lo, z, core), rep: 4 (over x).
Axes of the slice: x: 4, y: 4 (y_hi: 2, y_lo: 2; y = y_hi * 2 + y_lo), z: 4, core: 2. Of those that a mesh axis runs over, the one named last changes fastest.
Arguments:
- tokens: bfloat16 [2, 7168, 1024], P(None, ('shard', 'rep')), may hold values from -6 to 6
- segment_ids: int32 [2, 64, 112], P(None, ('shard', 'rep')), may hold values from 0 to 3, never falling along the last dimension, each value on 1 to 56 neighbouring positions
- cotangent: bfloat16 [2, 7168, 1024], P(None, ('shard', 'rep')), may hold values from -6 to 6
- norm_gains: bfloat16 [2, 1024, 2], P('section', 'shard'), may hold values from 0.5 to 1.5
- w_in: bfloat16 [2, 1024, 4120], P('section', 'shard'), may hold values from -0.1875 to 0.1875
- conv_params: bfloat16 [2, 1792, 5], P('section', 'shard'), may hold values from -1.5 to 1.5
- head_params: bfloat16 [2, 24, 3], P('section'), may hold values from -6.9 to 2.77, as said below
- w_out: bfloat16 [2, 2048, 1024], P('section', 'shard'), may hold values from -0.25 to 0.25
- w_gate_up: bfloat16 [2, 1024, 4096], P('section', 'shard'), may hold values from -0.1875 to 0.1875
- w_down: bfloat16 [2, 2048, 1024], P('section', 'shard'), may hold values from -0.125 to 0.125
Outputs:
- layer_out: bfloat16 [2, 2, 7168, 1024], P('section', None, ('shard', 'rep'))
- input_grads: float32 [2, 2, 7168, 1024], P('section', None, ('shard', 'rep'))
- grad_gains: float32 [2, 1024, 2], P('section', 'shard')
- grad_w_in: float32 [2, 1024, 4120], P('section', 'shard')
- grad_conv: float32 [2, 1792, 5], P('section', 'shard')
- grad_heads: float32 [2, 24, 3], P('section')
- grad_w_out: float32 [2, 2048, 1024], P('section', 'shard')
- grad_gate_up: float32 [2, 1024, 4096], P('section', 'shard')
- grad_w_down: float32 [2, 2048, 1024], P('section', 'shard')
Inputs may be any that keep to these rules, and one draw needn't show every extreme that they name: `segment_ids`: in each block of 112 slots the numbers never fall; each sequence holds 1 to 56 slots, and one holds exactly 56. `head_params`: column 0 (step bias) lies in -6.9 to -2.3, column 1 (log of the decay rate) in 0 to 2.77, column 2 (skip factor) in -1 to 1.
All inputs are finite; a program needn't handle non-finite values.
Results may differ from a plain program's by a relative error of at most 0.024.
Values may be sent and summed in bfloat16 or wider, within the bound.
A program may use at most 256 MiB of HBM per device.

v0:
```python
import math

import jax
import jax.numpy as jnp
from jax import lax
from jax.sharding import PartitionSpec as P

FF = 2048
MHEADS = 24
HEAD_WIDTH = 64
STATE = 128
QUERY_HEAD_COUNT = 8
KVHEADS = 2
CONV = 4
SSM = 1536
CH = 1792


def side_by_side(arrays, axis, dim, along):
    both = jnp.concatenate(arrays, axis=along)
    out, at, done = (lax.all_gather(both, axis, axis=dim, tiled=True), 0, [])
    for a in arrays:
        done.append(lax.slice_in_dim(out, at, at + a.shape[along], axis=along))
        at += a.shape[along]
    return tuple(done)


def from_behind(array, axis, by):
    size = lax.axis_size(axis)
    pairs = [(i, i + by) for i in range(size) if 0 <= i + by < size]
    return lax.ppermute(array, axis, pairs)


def sent_together(arrays, axis, dim, along):
    both = jnp.concatenate(arrays, axis=along)
    out, at, done = (lax.psum_scatter(both, axis, scatter_dimension=dim, tiled=True), 0, [])
    for a in arrays:
        done.append(lax.slice_in_dim(out, at, at + a.shape[along], axis=along))
        at += a.shape[along]
    return tuple(done)


def sent_to_all(array, axis):
    size = lax.axis_size(axis)
    return lax.all_to_all(
        jnp.broadcast_to(array[None], (size, *array.shape)), axis, 0, 0, tiled=True
    )


def over_copies(array, axis):
    everything = sent_to_all(array, axis)
    return jnp.sum(everything, axis=0)


def rms_norm(values, gain):
    return values * lax.rsqrt(jnp.mean(values * values, -1, keepdims=True) + 1e-05) * gain


def mixers(projected, conv_table, head_table, segments):
    sequence_length = projected.shape[0]
    exact_result = lax.Precision.HIGHEST
    gate_z = projected[:, :SSM]
    conv_input = projected[:, SSM : SSM + CH]
    offset_qkv = SSM + CH
    query_rows = projected[:, offset_qkv : offset_qkv + QUERY_HEAD_COUNT * HEAD_WIDTH]
    key_rows = projected[
        :,
        offset_qkv
        + QUERY_HEAD_COUNT * HEAD_WIDTH : offset_qkv
        + (QUERY_HEAD_COUNT + KVHEADS) * HEAD_WIDTH,
    ]
    value_rows = projected[
        :,
        offset_qkv
        + (QUERY_HEAD_COUNT + KVHEADS) * HEAD_WIDTH : offset_qkv
        + (QUERY_HEAD_COUNT + 2 * KVHEADS) * HEAD_WIDTH,
    ]
    step_raw = projected[:, offset_qkv + (QUERY_HEAD_COUNT + 2 * KVHEADS) * HEAD_WIDTH :]
    mixed_in = conv_table[:, CONV] + conv_input * conv_table[:, 0]
    for offset in range(1, CONV):
        shifted = jnp.concatenate(
            [jnp.zeros((offset, CH), conv_input.dtype), conv_input[: sequence_length - offset]], 0
        )
        linked = jnp.concatenate(
            [jnp.zeros((offset,), bool), segments[offset:] == segments[: sequence_length - offset]]
        )
        mixed_in = mixed_in + jnp.where(linked[:, None], shifted, 0.0) * conv_table[:, offset]
    activated = jax.nn.silu(mixed_in)
    states = activated[:, :SSM].reshape(sequence_length, MHEADS, HEAD_WIDTH)
    inputs_b = activated[:, SSM : SSM + STATE]
    outputs_c = activated[:, SSM + STATE :]
    step_size = jax.nn.softplus(step_raw + head_table[:, 0])
    decay_log = -step_size * jnp.exp(head_table[:, 1])
    running = jnp.cumsum(decay_log, 0)
    places = jnp.arange(sequence_length)
    allowed = (segments[:, None] == segments[None, :]) & (places[:, None] >= places[None, :])
    distance = running[:, None, :] - running[None, :, :]
    kernel_rows = jnp.where(
        allowed[:, :, None], jnp.exp(jnp.where(allowed[:, :, None], distance, 0.0)), 0.0
    )
    intersection = jnp.dot(outputs_c, inputs_b.T, precision=exact_result)
    kernel_rows = kernel_rows * intersection[:, :, None] * step_size[None, :, :]
    ssm_out = (
        jnp.einsum("tsh,shp->thp", kernel_rows, states, precision=exact_result)
        + head_table[:, 2][None, :, None] * states
    )
    gated_out = ssm_out.reshape(sequence_length, SSM) * jax.nn.silu(gate_z)
    group_size = QUERY_HEAD_COUNT // KVHEADS
    query_head_rows = query_rows.reshape(sequence_length, KVHEADS, group_size, HEAD_WIDTH)
    key_head_rows = key_rows.reshape(sequence_length, KVHEADS, HEAD_WIDTH)
    value_head_rows = value_rows.reshape(sequence_length, KVHEADS, HEAD_WIDTH)
    attention_scores = jnp.einsum(
        "oxlc,mxc->xlom", query_head_rows, key_head_rows, precision=exact_result
    ) / math.sqrt(HEAD_WIDTH)
    attention_scores = jnp.where(allowed, attention_scores, -1e30)
    largest = jnp.max(attention_scores, -1, keepdims=True)
    exponent = jnp.exp(attention_scores - largest)
    attention_probabilities = exponent / jnp.sum(exponent, -1, keepdims=True)
    attended_values = jnp.einsum(
        "cynk,kcj->ncyj", attention_probabilities, value_head_rows, precision=exact_result
    ).reshape(sequence_length, QUERY_HEAD_COUNT * HEAD_WIDTH)
    return jnp.concatenate([gated_out, attended_values], 1)


def forward_product(left, weight):
    return jnp.dot(left, weight, preferred_element_type=jnp.float32)


def back_product(grad_rows, weight):
    return lax.dot_general(
        grad_rows, weight, (((1,), (1,)), ((), ())), preferred_element_type=jnp.float32
    )


def outer_sum(left, right):
    return lax.dot_general(
        left, right, (((0,), (0,)), ((), ())), preferred_element_type=jnp.float32
    )


def unpack(gathered, head_params):
    return (
        gathered[0][0].astype(jnp.float32),
        gathered[1][0],
        gathered[2][0].astype(jnp.float32),
        gathered[3][0],
        gathered[4][0],
        gathered[5][0],
        head_params[0].astype(jnp.float32),
    )


def layer_forward(inputs, segments, weights):
    gain_pair, w_in, conv_table, w_out, w_gate_up, w_down, head_table = weights
    normed = rms_norm(inputs, gain_pair[:, 0]).astype(jnp.bfloat16)
    projected = forward_product(normed, w_in)
    joined = mixers(projected, conv_table, head_table, segments)
    hidden = inputs + forward_product(joined.astype(jnp.bfloat16), w_out)
    normed_two = rms_norm(hidden, gain_pair[:, 1]).astype(jnp.bfloat16)
    gate_up = forward_product(normed_two, w_gate_up)
    activated = (jax.nn.silu(gate_up[:, :FF]) * gate_up[:, FF:]).astype(jnp.bfloat16)
    return (
        hidden + forward_product(activated, w_down),
        (inputs, projected, joined, hidden, gate_up),
    )


def layer_backward(grad_out, saved_rows, segments, weights):
    gain_pair, w_in, conv_table, w_out, w_gate_up, w_down, head_table = weights
    inputs, projected, joined, hidden, gate_up = saved_rows
    grad_ffn = grad_out.astype(jnp.bfloat16)
    gate_part = gate_up[:, :FF]
    up_part = gate_up[:, FF:]
    sigmoid_gate = jax.nn.sigmoid(gate_part)
    swish_gate = gate_part * sigmoid_gate
    activated = (swish_gate * up_part).astype(jnp.bfloat16)
    grad_act = back_product(grad_ffn, w_down)
    grad_gate = grad_act * up_part * sigmoid_gate * (1.0 + gate_part * (1.0 - sigmoid_gate))
    grad_up = grad_act * swish_gate
    grad_gate_up = jnp.concatenate([grad_gate, grad_up], 1).astype(jnp.bfloat16)
    normed_two, norm_pull_two = jax.vjp(
        lambda values_in, gain_in: rms_norm(values_in, gain_in), hidden, gain_pair[:, 1]
    )
    normed_two_low = normed_two.astype(jnp.bfloat16)
    grad_hidden_part, grad_gain_two = norm_pull_two(back_product(grad_gate_up, w_gate_up))
    grad_hidden = grad_out + grad_hidden_part
    grad_branch = grad_hidden.astype(jnp.bfloat16)
    grad_joined = back_product(grad_branch, w_out)
    mixed_out, mixer_pull = jax.vjp(
        lambda proj_in, conv_in, head_in: mixers(proj_in, conv_in, head_in, segments),
        projected,
        conv_table,
        head_table,
    )
    grad_projected, grad_conv, grad_head = mixer_pull(grad_joined)
    grad_proj_low = grad_projected.astype(jnp.bfloat16)
    normed, norm_pull_one = jax.vjp(
        lambda values_in, gain_in: rms_norm(values_in, gain_in), inputs, gain_pair[:, 0]
    )
    normed_low = normed.astype(jnp.bfloat16)
    grad_input_part, grad_gain_one = norm_pull_one(back_product(grad_proj_low, w_in))
    grad_input = grad_hidden + grad_input_part
    product_pairs = (
        (normed_low, grad_proj_low),
        (joined.astype(jnp.bfloat16), grad_branch),
        (normed_two_low, grad_gate_up),
        (activated, grad_ffn),
    )
    return (
        grad_input,
        product_pairs,
        jnp.stack([grad_gain_one, grad_gain_two], 1),
        grad_conv,
        grad_head,
    )


def body(
    tokens,
    segment_ids,
    cotangent,
    norm_gains,
    w_in,
    conv_params,
    head_params,
    w_out,
    w_gate_up,
    w_down,
):
    section_index = lax.axis_index("section")
    micro_count = tokens.shape[0]
    gathered = (
        *side_by_side((norm_gains, w_in), "shard", 1, 2),
        lax.all_gather(conv_params, "shard", axis=1, tiled=True),
        lax.all_gather(w_out, "shard", axis=1, tiled=True),
        lax.all_gather(w_gate_up, "shard", axis=1, tiled=True),
        lax.all_gather(w_down, "shard", axis=1, tiled=True),
    )
    weights = unpack(gathered, head_params)
    received = jnp.zeros(tokens.shape[1:], jnp.bfloat16)
    outputs = []
    kept_rows = []
    for tick_index in range(micro_count + 1):
        micro_index = jnp.clip(tick_index - section_index, 0, micro_count - 1)
        segments = lax.dynamic_index_in_dim(segment_ids[:, 0], micro_index, 0, keepdims=False)
        first_input = tokens[min(tick_index, micro_count - 1)].astype(jnp.float32)
        inputs = jnp.where(section_index == 0, first_input, received.astype(jnp.float32))
        result, saved_rows = layer_forward(inputs, segments, weights)
        outputs.append(result)
        kept_rows.append(saved_rows)
        if tick_index < micro_count:
            received = from_behind(result.astype(jnp.bfloat16), "section", 1)
    stacked_out = jnp.stack(outputs)
    layer_out = jnp.stack(
        [
            lax.dynamic_index_in_dim(stacked_out, micro_slot + section_index, 0, keepdims=False)
            for micro_slot in range(micro_count)
        ]
    ).astype(jnp.bfloat16)[None]
    kept_stack = tuple(
        (jnp.stack([saved_rows[member] for saved_rows in kept_rows]) for member in range(5))
    )
    coming = jnp.zeros(tokens.shape[1:], jnp.bfloat16)
    grads_in = []
    pair_lists = [[], [], [], []]
    gain_total = jnp.zeros((norm_gains.shape[1] * lax.axis_size("shard"), 2), jnp.float32)
    conv_total = jnp.zeros(
        (conv_params.shape[1] * lax.axis_size("shard"), conv_params.shape[2]), jnp.float32
    )
    head_total = jnp.zeros(head_params.shape[1:], jnp.float32)
    for tick_index in range(micro_count + 1):
        micro_raw = tick_index - 1 + section_index
        live_flag = ((micro_raw >= 0) & (micro_raw < micro_count)).astype(jnp.float32)
        micro_index = jnp.clip(micro_raw, 0, micro_count - 1)
        segments = lax.dynamic_index_in_dim(segment_ids[:, 0], micro_index, 0, keepdims=False)
        saved_slot = jnp.clip(tick_index - 1 + 2 * section_index, 0, micro_count)
        saved_rows = tuple(
            (
                lax.dynamic_index_in_dim(member, saved_slot, 0, keepdims=False)
                for member in kept_stack
            )
        )
        top_grad = cotangent[min(tick_index, micro_count - 1)].astype(jnp.float32)
        grad_out = jnp.where(section_index == 1, top_grad, coming.astype(jnp.float32)) * live_flag
        grad_input, product_pairs, gain_grad, conv_grad, head_grad = layer_backward(
            grad_out, saved_rows, segments, weights
        )
        grads_in.append(grad_input)
        for position in range(4):
            pair_lists[position].append(product_pairs[position])
        gain_total = gain_total + gain_grad
        conv_total = conv_total + conv_grad
        head_total = head_total + head_grad
        if tick_index < micro_count:
            coming = from_behind(grad_input.astype(jnp.bfloat16), "section", -1)
    stacked_grads = jnp.stack(grads_in)
    input_grads = jnp.stack(
        [
            lax.dynamic_index_in_dim(
                stacked_grads, micro_slot + 1 - section_index, 0, keepdims=False
            )
            for micro_slot in range(micro_count)
        ]
    )[None]
    summed = []
    for position in range(4):
        left_rows = jnp.concatenate([entry[0] for entry in pair_lists[position]], 0)
        right_rows = jnp.concatenate([entry[1] for entry in pair_lists[position]], 0)
        summed.append(outer_sum(left_rows, right_rows))
    bundle = (
        gain_total[None],
        summed[0][None],
        conv_total[None],
        summed[1][None],
        summed[2][None],
        summed[3][None],
    )
    owned = (
        *tuple(
            (
                part.astype(jnp.float32)
                for part in sent_together(
                    (bundle[0].astype(jnp.bfloat16), bundle[1].astype(jnp.bfloat16)), "shard", 1, 2
                )
            )
        ),
        lax.psum_scatter(
            bundle[2].astype(jnp.bfloat16), "shard", scatter_dimension=1, tiled=True
        ).astype(jnp.float32),
        lax.psum_scatter(
            bundle[3].astype(jnp.bfloat16), "shard", scatter_dimension=1, tiled=True
        ).astype(jnp.float32),
        lax.psum_scatter(
            bundle[4].astype(jnp.bfloat16), "shard", scatter_dimension=1, tiled=True
        ).astype(jnp.float32),
        lax.psum_scatter(
            bundle[5].astype(jnp.bfloat16), "shard", scatter_dimension=1, tiled=True
        ).astype(jnp.float32),
    )
    reduced = (
        lax.psum(owned[0].astype(jnp.bfloat16), "rep").astype(jnp.float32),
        lax.psum(owned[1].astype(jnp.bfloat16), "rep").astype(jnp.float32),
        lax.psum(owned[2].astype(jnp.bfloat16), "rep").astype(jnp.float32),
        lax.psum(owned[3].astype(jnp.bfloat16), "rep").astype(jnp.float32),
        lax.psum(owned[4].astype(jnp.bfloat16), "rep").astype(jnp.float32),
        lax.psum(owned[5].astype(jnp.bfloat16), "rep").astype(jnp.float32),
    )
    head_sum = over_copies(head_total[None], ("shard", "rep"))
    return (
        layer_out,
        input_grads,
        reduced[0],
        reduced[1],
        reduced[2],
        head_sum,
        reduced[3],
        reduced[4],
        reduced[5],
    )


def solution(mesh):
    in_specs = (
        P(None, ("shard", "rep"), None),
        P(None, ("shard", "rep"), None),
        P(None, ("shard", "rep"), None),
        P("section", "shard", None),
        P("section", "shard", None),
        P("section", "shard", None),
        P("section", None, None),
        P("section", "shard", None),
        P("section", "shard", None),
        P("section", "shard", None),
    )
    out_specs = (
        P("section", None, ("shard", "rep"), None),
        P("section", None, ("shard", "rep"), None),
        P("section", "shard", None),
        P("section", "shard", None),
        P("section", "shard", None),
        P("section", None, None),
        P("section", "shard", None),
        P("section", "shard", None),
        P("section", "shard", None),
    )
    return jax.shard_map(body, mesh=mesh, in_specs=in_specs, out_specs=out_specs, check_vma=False)
```

profile of v0, /device:TPU:1, one launch (start us, length us, event | category | flops | bytes accessed | tf_op | source)
XLA Modules:
  0.0 1089.3 jit_solution(6327598379152842008)
XLA Ops:
  19.0 29.9 %all_gather.15 = bf16[1,1792,5]{2,0,1:T(2,128)(2,1)S(1)} all-gather(bf16[1,112,5]{2,0,1:T(2,128)(2,1)S(1)} %copy.389), channel_id=1, replica_groups=mesh['section'=2,'shard'=16,'rep'=4] {'shard'}, dimensions={1}, use_global_device_ids=true | all-gather | bytes 19040 | tf_op jit(solution)/shard_map/all_gather | solution.py:234
  60.6 10.5 all-gather.5.cloned.1.call-done
  96.2 15.9 %all-gather.7.cloned.1.call-done = bf16[1,2048,1024]{2,1,0:T(8,128)(2,1)} async-done(((bf16[1,128,1024]{2,1,0:T(8,128)(2,1)}), bf16[1,2048,1024]{2,1,0:T(8,128)(2,1)}) %all-gather.7.cloned.1.call-update) | async-done | bytes 4194320 | tf_op jit(solution)/shard_map/all_gather | solution.py:235
  115.2 50.9 %all-gather.9.cloned.1.call-done = bf16[1,1024,4096]{2,1,0:T(8,128)(2,1)} async-done(((bf16[1,64,4096]{2,1,0:T(8,128)(2,1)}), bf16[1,1024,4096]{2,1,0:T(8,128)(2,1)}) %all-gather.9.cloned.1.call-update) | async-done | bytes 8388624 | tf_op jit(solution)/shard_map/all_gather | solution.py:236
  172.5 33.6 %all-gather.11.cloned.1.call-done = bf16[1,2048,1024]{2,1,0:T(8,128)(2,1)} async-done(((bf16[1,128,1024]{2,1,0:T(8,128)(2,1)}), bf16[1,2048,1024]{2,1,0:T(8,128)(2,1)}) %all-gather.11.cloned.1.call-update) | async-done | bytes 4194320 | tf_op jit(solution)/shard_map/all_gather | solution.py:237
  226.8 6.2 fusion.41
  405.5 7.3 multiply_reduce_fusion.26
  454.3 7.2 multiply_reduce_fusion.23
  511.6 7.3 multiply_reduce_fusion.24
  541.2 7.8 multiply_reduce_fusion.21
  591.0 8.4 multiply_reduce_fusion.22
  599.5 7.4 fusion.12
  607.0 9.4 pad_maximum_fusion
  616.4 36.7 %copy.504 = bf16[1,1024,4122]{2,0,1:T(2,128)(2,1)} copy(bf16[1,1024,4122]{1,2,0:T(8,128)(2,1)} %pad_maximum_fusion) | data formatting | bytes 16883712
  653.1 11.5 %copy.512 = bf16[1024,1,4122]{2,0,1:T(8,128)(2,1)} copy(bf16[1024,1,4122]{2,1,0:T(2,128)(2,1)} %bitcast.749) | data formatting | bytes 16883712
  680.0 9.3 convert_bitcast_fusion
  704.7 34.3 %reduce-scatter.16.cloned.1.call-done = bf16[64,4122]{1,0:T(8,128)(2,1)} async-done(((bf16[1024,4122]{1,0:T(8,128)(2,1)}), bf16[64,4122]{1,0:T(8,128)(2,1)}) %reduce-scatter.16.cloned.1.call-update) | async-done | bytes 527632
  745.0 61.5 %reduce-scatter.10.cloned.1.call-done = bf16[1,128,1024]{2,1,0:T(8,128)(2,1)} async-done(((bf16[1,2048,1024]{2,1,0:T(8,128)(2,1)}), bf16[1,128,1024]{2,1,0:T(8,128)(2,1)}) %reduce-scatter.10.cloned.1.call-update) | async-done | bytes 262160 | tf_op jit(solution)/shard_map/reduce_scatter | solution.py:330
  806.5 67.9 %reduce-scatter.14.cloned.1.call-done = bf16[1,128,1024]{2,1,0:T(8,128)(2,1)} async-done(((bf16[1,2048,1024]{2,1,0:T(8,128)(2,1)}), bf16[1,128,1024]{2,1,0:T(8,128)(2,1)}) %reduce-scatter.14.cloned.1.call-update) | async-done | bytes 262160 | tf_op jit(solution)/shard_map/reduce_scatter | solution.py:336
  874.4 75.9 %reduce-scatter.12.cloned.1.call-done = bf16[1,64,4096]{2,1,0:T(8,128)(2,1)} async-done(((bf16[1,1024,4096]{2,1,0:T(8,128)(2,1)}), bf16[1,64,4096]{2,1,0:T(8,128)(2,1)}) %reduce-scatter.12.cloned.1.call-update) | async-done | bytes 524304 | tf_op jit(solution)/shard_map/reduce_scatter | solution.py:333
  953.1 9.2 all-to-all-start
  971.4 41.2 %reduce-scatter.18.cloned.1.call-done = bf16[112,5]{1,0:T(8,128)(2,1)} async-done(((bf16[1792,5]{1,0:T(8,128)(2,1)}), bf16[112,5]{1,0:T(8,128)(2,1)}) %reduce-scatter.18.cloned.1.call-update) | async-done | bytes 1136
  1013.9 8.5 all-reduce.90
  1023.5 53.6 %all-reduce.94.cloned.1.call-done = (bf16[1,64,4120]{1,2,0:T(8,128)(2,1)}, bf16[1,128,1024]{2,1,0:T(8,128)(2,1)}, bf16[1,64,4096]{2,1,0:T(8,128)(2,1)}, bf16[1,128,1024]{2,1,0:T(8,128)(2,1)}) async-done(((bf16[1,64,4120]{1,2,0:T(8,128)(2,1)}, bf16[1,128,1024]{2,1,0:T(8,128)(2,1)}, bf16[1,64,4096]{2,1,0:T(8,128)(2,1)}, bf16[1,128,1024]{2,1,0:T(8,128)(2,1)}), (bf16[1,64,4120]{1,2,0:T(8,128)(2,1)}, ...) | async-done | bytes 1575952 | tf_op jit(solution)/shard_map/psum | solution.py:342
  (1085 shorter events, 459.4 us)
Async XLA Ops:
  7.2 63.9 %all-gather.5.cloned.1.call-start = ((), (), s32[]{:S(2)}) async-start(), calls=%async_computation.6 | async-start | bytes 9191424 | tf_op jit(solution)/shard_map/all_gather | solution.py:21
  10.1 102.1 %all-gather.7.cloned.1.call-start = ((), (), s32[]{:S(2)}) async-start(), calls=%async_computation.7 | async-start | bytes 4456448 | tf_op jit(solution)/shard_map/all_gather | solution.py:235
  10.9 155.3 %all-gather.9.cloned.1.call-start = ((), (), s32[]{:S(2)}) async-start(), calls=%async_computation.8 | async-start | bytes 8912896 | tf_op jit(solution)/shard_map/all_gather | solution.py:236
  11.6 194.5 %all-gather.11.cloned.1.call-start = ((), (), s32[]{:S(2)}) async-start(), calls=%async_computation.9 | async-start | bytes 4456448 | tf_op jit(solution)/shard_map/all_gather | solution.py:237
  12.2 726.8 %reduce-scatter.16.cloned.1.call-start = ((), (), s32[]{:S(2)}) async-start(), calls=%async_computation.13 | async-start | bytes 9191424
  72.5 197.0 %copy-start.174 = (f32[1024]{0:T(1024)}, f32[1024]{0:T(1024)S(1)}, u32[]{:S(2)}) copy-start(f32[1024]{0:T(1024)S(1)} %get-tuple-element.115) | copy-start | bytes 12292
  115.2 90.9 %copy-start.40 = (f32[112,1024]{1,0:T(8,128)}, f32[112,1024]{1,0:T(8,128)S(1)}, u32[]{:S(2)}) copy-start(f32[112,1024]{1,0:T(8,128)S(1)} %get-tuple-element.257) | copy-start | bytes 1376260
  172.4 50.0 %copy-start.252 = (pred[112]{0:T(512)(128)(4,1)S(1)}, pred[112]{0:T(512)(128)(4,1)}, u32[]{:S(2)}) copy-start(pred[112]{0:T(512)(128)(4,1)} %pad_add_fusion.1) | copy-start | bytes 340
  172.4 50.6 %copy-start.188 = (pred[112,112]{1,0:T(8,128)(4,1)S(1)}, pred[112,112]{1,0:T(8,128)(4,1)}, u32[]{:S(2)}) copy-start(pred[112,112]{1,0:T(8,128)(4,1)} %get-tuple-element.251) | copy-start | bytes 37636
  172.5 51.3 %copy-start.247 = (pred[112]{0:T(512)(128)(4,1)S(1)}, pred[112]{0:T(512)(128)(4,1)}, u32[]{:S(2)}) copy-start(pred[112]{0:T(512)(128)(4,1)} %pad_add_fusion) | copy-start | bytes 340
  172.5 51.9 %copy-start.185 = (pred[112,112]{1,0:T(8,128)(4,1)S(1)}, pred[112,112]{1,0:T(8,128)(4,1)}, u32[]{:S(2)}) copy-start(pred[112,112]{1,0:T(8,128)(4,1)} %get-tuple-element.249) | copy-start | bytes 37636
  172.5 52.6 %copy-start.318 = (pred[111]{0:T(512)(128)(4,1)S(1)}, pred[111]{0:T(512)(128)(4,1)}, u32[]{:S(2)}) copy-start(pred[111]{0:T(512)(128)(4,1)} %compare_bitcast_fusion.14) | copy-start | bytes 337
  172.5 52.7 %copy-start.294 = (pred[111]{0:T(512)(128)(4,1)S(1)}, pred[111]{0:T(512)(128)(4,1)}, u32[]{:S(2)}) copy-start(pred[111]{0:T(512)(128)(4,1)} %get-tuple-element.289) | copy-start | bytes 337
  209.7 16.2 %collective-permute-start = (bf16[112,1024]{1,0:T(8,128)(2,1)S(1)}, bf16[112,1024]{1,0:T(8,128)(2,1)S(1)}, u32[]{:S(2)}, u32[]{:S(2)}) collective-permute-start(bf16[112,1024]{1,0:T(8,128)(2,1)S(1)} %fusion.174), channel_id=1, source_target_pairs={{0,64},{1,65},{2,66},{3,67},{4,68},{5,69},{6,70},{7,71},{8,72},{9,... | collective-permute-start | bytes 688136 | tf_op jit(solution)/shard_map/ppermute | solution.py:31
  262.5 6.1 collective-permute-start.1
  414.0 33.9 %collective-permute-start.2 = (bf16[112,1024]{1,0:T(8,128)(2,1)}, bf16[112,1024]{1,0:T(8,128)(2,1)}, u32[]{:S(2)}, u32[]{:S(2)}) collective-permute-start(bf16[112,1024]{1,0:T(8,128)(2,1)} %get-tuple-element.157), channel_id=1, source_target_pairs={{64,0},{65,1},{66,2},{67,3},{68,4},{69,5},{70,6},{71,7},{72,8},{73... | collective-permute-start | bytes 688136 | tf_op jit(solution)/shard_map/ppermute | solution.py:31
  520.0 14.9 %collective-permute-start.3 = (bf16[112,1024]{1,0:T(8,128)(2,1)}, bf16[112,1024]{1,0:T(8,128)(2,1)S(1)}, u32[]{:S(2)}, u32[]{:S(2)}) collective-permute-start(bf16[112,1024]{1,0:T(8,128)(2,1)} %get-tuple-element.149), channel_id=1, source_target_pairs={{64,0},{65,1},{66,2},{67,3},{68,4},{69,5},{70,6},{71,7},{72,8},{73... | collective-permute-start | bytes 688136 | tf_op jit(solution)/shard_map/ppermute | solution.py:31
  664.6 141.9 %reduce-scatter.10.cloned.1.call-start = ((), (), s32[]{:S(2)}) async-start(), calls=%async_computation.10 | async-start | bytes 4456448 | tf_op jit(solution)/shard_map/reduce_scatter | solution.py:330
  671.7 202.7 %reduce-scatter.14.cloned.1.call-start = ((), (), s32[]{:S(2)}) async-start(), calls=%async_computation.12 | async-start | bytes 4456448 | tf_op jit(solution)/shard_map/reduce_scatter | solution.py:336
  678.6 271.8 %reduce-scatter.12.cloned.1.call-start = ((), (), s32[]{:S(2)}) async-start(), calls=%async_computation.11 | async-start | bytes 8912896 | tf_op jit(solution)/shard_map/reduce_scatter | solution.py:333
  689.4 323.2 %reduce-scatter.18.cloned.1.call-start = ((), (), s32[]{:S(2)}) async-start(), calls=%async_computation.14 | async-start | bytes 487424
  704.6 372.5 %all-reduce.94.cloned.1.call-start = ((), (), s32[]{:S(2)}) async-start(), calls=%async_computation.15 | async-start | bytes 4206592 | tf_op jit(solution)/shard_map/psum | solution.py:342
  745.0 205.4 %copy-start.71 = (bf16[3,112,1024]{2,1,0:T(8,128)(2,1)S(1)}, bf16[3,112,1024]{2,1,0:T(8,128)(2,1)}, u32[]{:S(2)}) copy-start(bf16[3,112,1024]{2,1,0:T(8,128)(2,1)} %pad_maximum_fusion.4) | copy-start | bytes 2064388
  953.1 17.6 %all-to-all-start = ((f32[64,1,24,3]{2,1,3,0:T(1,128)}), f32[64,1,24,3]{2,1,3,0:T(1,128)S(1)}, u32[]{:S(2)}, u32[]{:S(2)}) async-start(f32[64,1,24,3]{2,1,3,0:T(1,128)} %broadcast_in_dim.552), calls=%async_computation | async-start | bytes 196608 | tf_op jit(solution)/shard_map/all_to_all | solution.py:45
  (324 other events, 2271.5 us)
Sparse Core Ops, SparseCore 0:
  10.3 60.6 all-gather.4
  72.8 39.3 all-gather.6
  113.9 52.2 all-gather.8
  167.7 38.3 all-gather.10
  664.7 74.1 reduce-scatter.15
  741.3 65.1 reduce-scatter.9
  809.1 65.2 reduce-scatter.13
  876.9 73.3 reduce-scatter.11
  953.4 59.1 reduce-scatter.17
  1015.6 61.4 all-reduce.93
where the time goes:
time: 1100 us; the launch traced here: 1090 us
  waiting for transfers between devices  456 us (41%)
  matrix products  235 us (21%)
  local copies, waits for them, and re-layouts  201 us (18%)
  other arithmetic  122 us (11%)
  blocking collectives  38.4 us (3%)
  starting transfers between devices  19 us (2%)
  between operations  18.4 us (2%)
    unnamed x669, local copies, waits for them, and re-layouts  88 us
    unnamed x12, waiting for transfers between devices  77.4 us
    reduce_scatter x1, waiting for transfers between devices, body(): lax.psum_scatter(bundle[4].astype(jnp.bfloat16), 'shard', scatter_dimensi...  75.9 us
    reduce_scatter x1, waiting for transfers between devices, body(): lax.psum_scatter(bundle[5].astype(jnp.bfloat16), 'shard', scatter_dimensi...  67.9 us
    dot_general x12, matrix products, back_product(): lax.dot_general(grad_rows, weight, (((1,), (1,)), ((), ())), preferred_el...  62 us
    reduce_scatter x1, waiting for transfers between devices, body(): lax.psum_scatter(bundle[3].astype(jnp.bfloat16), 'shard', scatter_dimensi...  61.5 us
    dot_general x12, matrix products, mixers(): jnp.einsum('tsh,shp->thp', kernel_rows, states, precision=exact_result)  56 us
    psum x1, waiting for transfers between devices, body(): lax.psum(owned[1].astype(jnp.bfloat16), 'rep').astype(jnp.float32)  53.6 us
  transfers between devices with their start and end apart: 15, of which 12 were waited for; matrix products, arithmetic and copies ran while one was open for 14% of the time, Pallas kernels for 0%

commit v1 on v0

v1 whole, which is shorter than its diff:
```python
import functools
import math

import jax
import jax.numpy as jnp
from jax import lax
from jax.experimental import pallas as pl
from jax.experimental.pallas import tpu as pltpu
from jax.sharding import PartitionSpec as P

FF = 2048
MHEADS = 24
HEAD_WIDTH = 64
STATE = 128
QUERY_HEAD_COUNT = 8
KVHEADS = 2
CONV = 4
SSM = 1536
CH = 1792
UW = 2048
PIN = 4120
PAD = 4224
T = 112
OFF_Q = SSM + CH
OFF_K = OFF_Q + QUERY_HEAD_COUNT * HEAD_WIDTH
OFF_V = OFF_K + KVHEADS * HEAD_WIDTH
OFF_R = OFF_V + KVHEADS * HEAD_WIDTH
F32 = jnp.float32
BF16 = jnp.bfloat16


def dot_nn(left, right):
    return jnp.dot(left.astype(BF16), right.astype(BF16), preferred_element_type=F32)


def dot_nt(left, right):
    return lax.dot_general(
        left.astype(BF16), right.astype(BF16), (((1,), (1,)), ((), ())), preferred_element_type=F32
    )


def dot_tn(left, right):
    return lax.dot_general(
        left.astype(BF16), right.astype(BF16), (((0,), (0,)), ((), ())), preferred_element_type=F32
    )


def exact_dot(left, right):
    return jnp.dot(left, right, precision=lax.Precision.HIGHEST, preferred_element_type=F32)


def iota(shape, dim):
    return lax.broadcasted_iota(jnp.int32, shape, dim)


def block_masks(segc, segr):
    rows, cols = iota((T, T), 0), iota((T, T), 1)
    allowed = (segc[:, :T] == segr[0:1, :]) & (rows >= cols)
    places = iota((T, 128), 0)
    links = [
        jnp.where((pltpu.roll(segc, j, 0) == segc) & (places >= j), 1.0, 0.0)
        for j in range(1, CONV)
    ]
    return allowed, links


def convolve(p_ref, conv_ref, links, mixed_ref, act_ref):
    for at in range(0, CH, 128):
        sl = slice(at, at + 128)
        c = p_ref[0, :, SSM + at : SSM + at + 128]
        mixed = conv_ref[4:5, sl] + c * conv_ref[0:1, sl]
        for j in range(1, CONV):
            mixed = mixed + links[j - 1] * pltpu.roll(c, j, 0) * conv_ref[j : j + 1, sl]
        if mixed_ref is not None:
            mixed_ref[:, sl] = mixed
        act_ref[:, sl] = mixed * jax.nn.sigmoid(mixed)


def softplus(v):
    return jnp.maximum(v, 0.0) + jnp.log1p(jnp.exp(-jnp.abs(v)))


def steps_and_sums(p_ref, head_ref):
    raw = p_ref[0, :, OFF_R:PAD] + head_ref[0:1, :]
    live = iota((T, 128), 1) < MHEADS
    raw = jnp.where(live, raw, 0.0)
    dt = softplus(raw)
    decay = -dt * jnp.exp(head_ref[1:2, :])
    lower = jnp.where(iota((T, T), 0) >= iota((T, T), 1), 1.0, 0.0)
    return raw, dt, decay, exact_dot(lower, decay)


def attention_probs(q_tile, keep, k_dup, allowed):
    scores = dot_nt(jnp.where(keep, q_tile, 0.0), k_dup) * (1.0 / math.sqrt(HEAD_WIDTH))
    scores = jnp.where(allowed, scores, -1e30)
    e = jnp.exp(scores - jnp.max(scores, -1, keepdims=True))
    return e / jnp.sum(e, -1, keepdims=True)


def doubled(tile, left):
    turned = pltpu.roll(tile, HEAD_WIDTH, 1)
    return jnp.where(left, tile, turned), jnp.where(left, turned, tile)


def mix_forward_kernel(p_ref, segc_ref, segr_ref, conv_ref, head_ref, skip_ref, u_ref, act_ref):
    allowed, links = block_masks(segc_ref[0], segr_ref[0])
    convolve(p_ref, conv_ref, links, None, act_ref)
    _, dt, _, cum = steps_and_sums(p_ref, head_ref)
    dt_t, cum_t = dt.T, cum.T
    left = iota((T, 128), 1) < HEAD_WIDTH
    cb = dot_nt(act_ref[:, SSM + STATE :], act_ref[:, SSM : SSM + STATE])
    for pair in range(MHEADS // 2):
        sl = slice(128 * pair, 128 * pair + 128)
        xs = act_ref[:, sl]
        ys = []
        for h in (2 * pair, 2 * pair + 1):
            decayed = jnp.exp(jnp.where(allowed, cum[:, h : h + 1] - cum_t[h : h + 1, :], -1e30))
            ys.append(dot_nn(decayed * cb * dt_t[h : h + 1, :], xs))
        y = jnp.where(left, ys[0], ys[1]) + skip_ref[0:1, sl] * xs
        z = p_ref[0, :, sl]
        u_ref[0, :, sl] = (y * (z * jax.nn.sigmoid(z))).astype(BF16)
    k_dups = doubled(p_ref[0, :, OFF_K:OFF_V], left)
    v_dups = doubled(p_ref[0, :, OFF_V:OFF_R], left)
    for pair in range(QUERY_HEAD_COUNT // 2):
        kv = pair // 2
        q_tile = p_ref[0, :, OFF_Q + 128 * pair : OFF_Q + 128 * pair + 128]
        probs = [attention_probs(q_tile, keep, k_dups[kv], allowed) for keep in (left, ~left)]
        out = [dot_nn(pr, v_dups[kv]) for pr in probs]
        u_ref[0, :, SSM + 128 * pair : SSM + 128 * pair + 128] = jnp.where(
            left, out[0], out[1]
        ).astype(BF16)


def mix_backward_kernel(
    p_ref, gu_ref, segc_ref, segr_ref, conv_ref, head_ref, skip_ref,
    gp_ref, gconv_ref, ghead_ref, gskip_ref,
    mixed_ref, act_ref, gact_ref, colq_ref,
):
    allowed, links = block_masks(segc_ref[0], segr_ref[0])
    convolve(p_ref, conv_ref, links, mixed_ref, act_ref)
    raw, dt, decay, cum = steps_and_sums(p_ref, head_ref)
    dt_t, cum_t = dt.T, cum.T
    lanes = iota((T, 128), 1)
    left = lanes < HEAD_WIDTH
    b_rows = act_ref[:, SSM : SSM + STATE]
    c_rows = act_ref[:, SSM + STATE :]
    cb = dot_nt(c_rows, b_rows)
    gcb = jnp.zeros((T, T), F32)
    row_form = jnp.zeros((T, 128), F32)
    colq_ref[...] = jnp.zeros_like(colq_ref)
    for pair in range(MHEADS // 2):
        sl = slice(128 * pair, 128 * pair + 128)
        xs = act_ref[:, sl]
        xs16 = xs.astype(BF16)
        z = p_ref[0, :, sl]
        gm = gu_ref[0, :, sl]
        sg = jax.nn.sigmoid(z)
        gy = gm * (z * sg)
        gy16 = gy.astype(BF16)
        ys, gxs = [], []
        for h, keep in ((2 * pair, left), (2 * pair + 1, ~left)):
            decayed = jnp.exp(jnp.where(allowed, cum[:, h : h + 1] - cum_t[h : h + 1, :], -1e30))
            dt_row = dt_t[h : h + 1, :]
            base = decayed * cb
            k16 = (base * dt_row).astype(BF16)
            ys.append(dot_nn(k16, xs16))
            gxs.append(dot_tn(k16, gy16))
            gk = dot_nt(jnp.where(keep, gy, 0.0), xs16)
            gcb = gcb + gk * (decayed * dt_row)
            q = gk * base
            colq_ref[h : h + 1, :] = jnp.sum(q, 0, keepdims=True)
            row_form = jnp.where(lanes == h, jnp.sum(q * dt_row, 1, keepdims=True), row_form)
        skip = skip_ref[0:1, sl]
        y = jnp.where(left, ys[0], ys[1]) + skip * xs
        gp_ref[0, :, sl] = (gm * y * (sg * (1.0 + z * (1.0 - sg)))).astype(BF16)
        gact_ref[:, sl] = jnp.where(left, gxs[0], gxs[1]) + skip * gy
        gskip_ref[0, 0:1, sl] = jnp.sum(gy * xs, 0, keepdims=True)
    gact_ref[:, SSM : SSM + STATE] = dot_tn(gcb, c_rows)
    gact_ref[:, SSM + STATE :] = dot_nn(gcb, b_rows)
    col_form = colq_ref[...].T
    gcum = row_form - col_form * dt
    upper = jnp.where(iota((T, T), 0) <= iota((T, T), 1), 1.0, 0.0)
    gdecay = exact_dot(upper, gcum)
    gdt = col_form - gdecay * jnp.exp(head_ref[1:2, :])
    graw = jnp.where(lanes < MHEADS, gdt * jax.nn.sigmoid(raw), 0.0)
    gp_ref[0, :, OFF_R:PAD] = graw.astype(BF16)
    ghead_ref[0, 0:1, :] = jnp.sum(graw, 0, keepdims=True)
    ghead_ref[0, 1:2, :] = jnp.sum(gdecay * decay, 0, keepdims=True)
    for at in range(0, CH, 128):
        sl = slice(at, at + 128)
        mixed = mixed_ref[:, sl]
        sg = jax.nn.sigmoid(mixed)
        gmix = gact_ref[:, sl] * (sg * (1.0 + mixed * (1.0 - sg)))
        c = p_ref[0, :, SSM + at : SSM + at + 128]
        gc = gmix * conv_ref[0:1, sl]
        gconv_ref[0, 0:1, sl] = jnp.sum(gmix * c, 0, keepdims=True)
        for j in range(1, CONV):
            linked = gmix * links[j - 1]
            gc = gc + pltpu.roll(linked, T - j, 0) * conv_ref[j : j + 1, sl]
            gconv_ref[0, j : j + 1, sl] = jnp.sum(linked * pltpu.roll(c, j, 0), 0, keepdims=True)
        gconv_ref[0, 4:5, sl] = jnp.sum(gmix, 0, keepdims=True)
        gp_ref[0, :, SSM + at : SSM + at + 128] = gc.astype(BF16)
    k_dups = doubled(p_ref[0, :, OFF_K:OFF_V], left)
    v_dups = doubled(p_ref[0, :, OFF_V:OFF_R], left)
    gks, gvs = [], []
    for kv in range(KVHEADS):
        gk_sum = jnp.zeros((T, 128), F32)
        gv_sum = jnp.zeros((T, 128), F32)
        for pair in (2 * kv, 2 * kv + 1):
            sl = slice(OFF_Q + 128 * pair, OFF_Q + 128 * pair + 128)
            q_tile = p_ref[0, :, sl]
            go = gu_ref[0, :, SSM + 128 * pair : SSM + 128 * pair + 128]
            gq, gk, gv = [], [], []
            for keep in (left, ~left):
                probs = attention_probs(q_tile, keep, k_dups[kv], allowed)
                gpr = dot_nt(jnp.where(keep, go, 0.0), v_dups[kv])
                gs = probs * (gpr - jnp.sum(gpr * probs, -1, keepdims=True))
                gs = (gs * (1.0 / math.sqrt(HEAD_WIDTH))).astype(BF16)
                gq.append(dot_nn(gs, k_dups[kv]))
                gk.append(dot_tn(gs, q_tile))
                gv.append(dot_tn(probs, go))
            gp_ref[0, :, sl] = jnp.where(left, gq[0], gq[1]).astype(BF16)
            gk_sum = gk_sum + jnp.where(left, gk[0], gk[1])
            gv_sum = gv_sum + jnp.where(left, gv[0], gv[1])
        gks.append(gk_sum + pltpu.roll(gk_sum, HEAD_WIDTH, 1))
        gvs.append(gv_sum + pltpu.roll(gv_sum, HEAD_WIDTH, 1))
    gp_ref[0, :, OFF_K:OFF_V] = jnp.where(left, gks[0], gks[1]).astype(BF16)
    gp_ref[0, :, OFF_V:OFF_R] = jnp.where(left, gvs[0], gvs[1]).astype(BF16)


def whole(shape):
    return pl.BlockSpec(shape, lambda m: (0,) * len(shape))


def per_block(shape):
    return pl.BlockSpec((1, *shape), lambda m: (m,) + (0,) * len(shape))


def small_specs():
    return [
        per_block((T, 128)), per_block((8, T)), whole((8, CH)), whole((8, 128)), whole((8, SSM)),
    ]


def mix_forward(projected, tables):
    blocks = projected.shape[0]
    return pl.pallas_call(
        mix_forward_kernel,
        grid=(blocks,),
        in_specs=[per_block((T, PAD)), *small_specs()],
        out_specs=per_block((T, UW)),
        out_shape=jax.ShapeDtypeStruct((blocks, T, UW), BF16),
        scratch_shapes=[pltpu.VMEM((T, CH), F32)],
        compiler_params=pltpu.CompilerParams(vmem_limit_bytes=32 * 1024 * 1024),
        name="mix_forward",
    )(projected, *tables)


def mix_backward(projected, grad_joined, tables):
    blocks = projected.shape[0]
    return pl.pallas_call(
        mix_backward_kernel,
        grid=(blocks,),
        in_specs=[per_block((T, PAD)), per_block((T, UW)), *small_specs()],
        out_specs=[per_block((T, PAD)), per_block((8, CH)), per_block((8, 128)), per_block((8, SSM))],
        out_shape=[
            jax.ShapeDtypeStruct((blocks, T, PAD), BF16),
            jax.ShapeDtypeStruct((blocks, 8, CH), F32),
            jax.ShapeDtypeStruct((blocks, 8, 128), F32),
            jax.ShapeDtypeStruct((blocks, 8, SSM), F32),
        ],
        scratch_shapes=[
            pltpu.VMEM((T, CH), F32),
            pltpu.VMEM((T, CH), F32),
            pltpu.VMEM((T, CH), F32),
            pltpu.VMEM((128, T), F32),
        ],
        compiler_params=pltpu.CompilerParams(vmem_limit_bytes=40 * 1024 * 1024),
        name="mix_backward",
    )(projected, grad_joined, *tables)


def mixer_tables(segments, conv_table, head_table):
    blocks = segments.shape[0]
    marks = segments.astype(F32)
    segc = jnp.broadcast_to(marks[:, :, None], (blocks, T, 128))
    segr = jnp.broadcast_to(marks[:, None, :], (blocks, 8, T))
    conv_rows = jnp.pad(conv_table.T, ((0, 3), (0, 0)))
    head_rows = jnp.pad(head_table.T, ((0, 5), (0, 128 - MHEADS)))
    skip_rows = jnp.broadcast_to(jnp.repeat(head_table[:, 2], HEAD_WIDTH)[None], (8, SSM))
    return segc, segr, conv_rows, head_rows, skip_rows


MESH = pl.DeviceIdType.MESH
HOPS = ("xa", "xb", "za", "zb", "y")
PARTS = (
    (3, 0, 1024, ("y", "xa", "za", "xb", "zb")),
    (2, 0, 2048, ("za", "zb", "xa", "xb", "y")),
    (2, 2048, 2048, ("zb", "za", "xb", "xa", "y")),
    (1, 0, 1024, ("xa", "xb", "za", "zb", "y")),
    (0, 0, 2176, ("xb", "xa", "zb", "za", "y")),
    (0, 2176, 2048, ("y", "zb", "xb", "za", "xa")),
)
SHARD_ROWS = (64, 128, 64, 128)
SHARD_COLS = (PAD, 1024, 2 * FF, 1024)


def pair_a(i):
    return i + 1 - 2 * (i % 2)


def pair_b(i):
    return (i + 2 * (i % 2) + 3) % 4


def place():
    shard = lax.axis_index("shard")
    return lax.axis_index("section"), shard // 8, (shard // 2) % 4, shard % 2, lax.axis_index("rep")


def neighbours(section, y, z, core, x):
    def at(y, z, core, x):
        return (section, y * 8 + z * 2 + core, x)

    return {
        "core": at(y, z, 1 - core, x),
        "xa": at(y, z, core, pair_a(x)),
        "xb": at(y, z, core, pair_b(x)),
        "za": at(y, pair_a(z), core, x),
        "zb": at(y, pair_b(z), core, x),
        "y": at(1 - y, z, core, x),
        "xo": at(y, z, core, (x + 2) % 4),
    }


def meet(devices):
    barrier = pltpu.get_barrier_semaphore()
    for device in devices:
        pl.semaphore_signal(barrier, inc=1, device_id=device, device_id_type=MESH)
    pl.semaphore_wait(barrier, len(devices))


def halve(kept, hop, me):
    near, other = (pair_a, pair_b) if hop == "a" else (pair_b, pair_a)
    if len(kept) == 4:
        return [near(me), other(near(me))], [me, other(me)]
    return [near(me)], [me]


def schedule(order, me_y, me_z, me_x):
    every = [0, 1, 2, 3]
    ys, zs, xs = None, every, every
    stages = []

    def pieces(ys, zs, xs):
        zs = [None] if len(zs) == 4 else zs
        xs = [None] if len(xs) == 4 else xs
        return [(ys, z, x) for z in zs for x in xs]

    for hop in order:
        if hop == "y":
            stages.append((pieces(1 - me_y, zs, xs), pieces(me_y, zs, xs)))
            ys = me_y
        elif hop[0] == "z":
            sent, zs_kept = halve(zs, hop[1], me_z)
            stages.append((pieces(ys, sent, xs), pieces(ys, zs_kept, xs)))
            zs = zs_kept
        else:
            sent, xs_kept = halve(xs, hop[1], me_x)
            stages.append((pieces(ys, zs, sent), pieces(ys, zs, xs_kept)))
            xs = xs_kept
    return stages


def window(piece, quarter, column, columns):
    y, z, x = piece
    return (
        slice(0, 2) if y is None else pl.ds(y, 1),
        slice(0, 4) if z is None else pl.ds(z, 1),
        slice(0, 4 * quarter) if x is None else pl.ds(pl.multiple_of(x * quarter, quarter), quarter),
        pl.ds(column, columns),
    )


def piece_dims(piece, quarter):
    y, z, x = piece
    return (2 if y is None else 1, 4 if z is None else 1, 4 * quarter if x is None else quarter)


def stage_shapes():
    shapes = []
    for array, column, columns, order in PARTS:
        for sent, _ in schedule(order, 0, 0, 0):
            dims = piece_dims(sent[0], SHARD_ROWS[array] // 4)
            shapes.append((len(sent), *dims, columns))
    return shapes


def add_into(acc, window_at, arrived):
    ny, nz, rows, columns = arrived.shape
    ys, zs, rs, cs = window_at
    y0 = 0 if isinstance(ys, slice) else ys.start
    z0 = 0 if isinstance(zs, slice) else zs.start
    r0 = 0 if isinstance(rs, slice) else rs.start
    tiles = rows // 16

    def step(i, carry):
        y, rest = i // (nz * tiles), i % (nz * tiles)
        z, t = rest // tiles, rest % tiles
        row = pl.ds(pl.multiple_of(t * 16, 16), 16)
        at = (y0 + y, z0 + z, pl.ds(pl.multiple_of(r0 + t * 16, 16), 16), cs)
        acc[at] = acc[at] + arrived[y, z, row, :]
        return carry

    lax.fori_loop(0, ny * nz * tiles, step, 0)


def scatter_kernel(*refs):
    grads, outs = refs[:4], refs[4:8]
    accs, wholes, cores = refs[8:12], refs[12:16], refs[16:22]
    n_stage = len(PARTS) * len(HOPS)
    arrivals = refs[22 : 22 + n_stage]
    local_sem, core_send, core_recv, send_sem, recv_sem, last_send, last_recv = refs[22 + n_stage :]
    section, y, z, core, x = place()
    near = neighbours(section, y, z, core, x)
    meet([near[name] for name in ("core", *HOPS, "xo")])

    loads, swaps = [], []
    for p, (array, column, columns, _) in enumerate(PARTS):
        cols = pl.ds(column, columns)
        swap = pltpu.make_async_remote_copy(
            src_ref=grads[array].at[:, :, 1 - core, :, cols],
            dst_ref=cores[p],
            send_sem=core_send.at[p],
            recv_sem=core_recv.at[p],
            device_id=near["core"],
            device_id_type=MESH,
        )
        swap.start()
        load = pltpu.make_async_copy(
            grads[array].at[:, :, core, :, cols], accs[array].at[:, :, :, cols], local_sem.at[p]
        )
        load.start()
        swaps.append(swap)
        loads.append(load)

    plans = [schedule(order, y, z, x) for _, _, _, order in PARTS]
    flying = {}
    sems = 0
    for stage in range(len(HOPS) + 1):
        for p, (array, column, columns, order) in enumerate(PARTS):
            quarter = SHARD_ROWS[array] // 4
            if stage == 0:
                loads[p].wait()
                swaps[p].wait_recv()
                add_into(accs[array], window((None, None, None), quarter, column, columns), cores[p])
            else:
                kept = plans[p][stage - 1][1]
                for k, (copy, piece) in enumerate(zip(flying[p, stage - 1], kept)):
                    copy.wait_recv()
                    add_into(
                        accs[array],
                        window(piece, quarter, column, columns),
                        arrivals[p * len(HOPS) + stage - 1].at[k],
                    )
            if stage < len(HOPS):
                copies = []
                for k, piece in enumerate(plans[p][stage][0]):
                    copy = pltpu.make_async_remote_copy(
                        src_ref=accs[array].at[window(piece, quarter, column, columns)],
                        dst_ref=arrivals[p * len(HOPS) + stage].at[k],
                        send_sem=send_sem.at[sems],
                        recv_sem=recv_sem.at[sems],
                        device_id=near[order[stage]],
                        device_id_type=MESH,
                    )
                    copy.start()
                    copies.append(copy)
                    sems += 1
                flying[p, stage] = copies

    last = []
    for array in range(4):
        quarter = SHARD_ROWS[array] // 4
        mine = pl.ds(pl.multiple_of(x * quarter, quarter), quarter)
        for k, name in enumerate(("xo", "xa", "xb")):
            copy = pltpu.make_async_remote_copy(
                src_ref=accs[array].at[y, z, mine],
                dst_ref=wholes[array].at[mine],
                send_sem=last_send.at[array, k],
                recv_sem=last_recv.at[array, k],
                device_id=near[name],
                device_id_type=MESH,
            )
            copy.start()
            last.append(copy)
        outs[array][mine, :] = accs[array][y, z, mine, :].astype(F32)
    for array in range(4):
        quarter = SHARD_ROWS[array] // 4
        for k, owner in enumerate(((x + 2) % 4, pair_a(x), pair_b(x))):
            last[array * 3 + k].wait_recv()
            theirs = pl.ds(pl.multiple_of(owner * quarter, quarter), quarter)
            outs[array][theirs, :] = wholes[array][theirs, :].astype(F32)
    for copy in last + swaps + [c for copies in flying.values() for c in copies]:
        copy.wait_send()


def scatter_sums(grads):
    n_copies = sum(shape[0] for shape in stage_shapes())
    return pl.pallas_call(
        scatter_kernel,
        in_specs=[pl.BlockSpec(memory_space=pl.ANY)] * 4,
        out_specs=[pl.BlockSpec(memory_space=pltpu.VMEM)] * 4,
        out_shape=[jax.ShapeDtypeStruct(s, F32) for s in zip(SHARD_ROWS, SHARD_COLS)],
        scratch_shapes=[
            *[pltpu.VMEM((2, 4, r, c), BF16) for r, c in zip(SHARD_ROWS, SHARD_COLS)],
            *[pltpu.VMEM((r, c), BF16) for r, c in zip(SHARD_ROWS, SHARD_COLS)],
            *[pltpu.VMEM((2, 4, SHARD_ROWS[a], cols), BF16) for a, _, cols, _ in PARTS],
            *[pltpu.VMEM(shape, BF16) for shape in stage_shapes()],
            pltpu.SemaphoreType.DMA((len(PARTS),)),
            pltpu.SemaphoreType.DMA((len(PARTS),)),
            pltpu.SemaphoreType.DMA((len(PARTS),)),
            pltpu.SemaphoreType.DMA((n_copies,)),
            pltpu.SemaphoreType.DMA((n_copies,)),
            pltpu.SemaphoreType.DMA((4, 3)),
            pltpu.SemaphoreType.DMA((4, 3)),
        ],
        compiler_params=pltpu.CompilerParams(
            collective_id=1, has_side_effects=True, vmem_limit_bytes=58 * 1024 * 1024
        ),
        name="scatter_sums",
    )(*grads)


def rms_norm(values, gain):
    return values * lax.rsqrt(jnp.mean(values * values, -1, keepdims=True) + 1e-05) * gain


def rms_back(values, gain, grad):
    scale = lax.rsqrt(jnp.mean(values * values, -1, keepdims=True) + 1e-05)
    unit = values * scale
    scaled = grad * gain
    grad_values = scale * (scaled - unit * jnp.mean(scaled * unit, -1, keepdims=True))
    return grad_values, jnp.sum(grad * unit, 0)


def forward_product(left, weight):
    return jnp.dot(left, weight, preferred_element_type=F32)


def back_product(grad_rows, weight):
    return lax.dot_general(
        grad_rows, weight, (((1,), (1,)), ((), ())), preferred_element_type=F32
    )


def outer_sum(left, right):
    return lax.dot_general(
        left, right, (((0,), (0,)), ((), ())), preferred_element_type=F32
    ).astype(BF16)


def layer_forward(inputs, weights, tables):
    gains, w_in, w_out, w_gate_up, w_down = weights
    blocks = inputs.shape[0] // T
    normed = rms_norm(inputs, gains[0]).astype(BF16)
    projected = forward_product(normed, w_in)
    joined = mix_forward(projected.reshape(blocks, T, PAD), tables).reshape(blocks * T, UW)
    hidden = inputs + forward_product(joined, w_out)
    normed_two = rms_norm(hidden, gains[1]).astype(BF16)
    gate_up = forward_product(normed_two, w_gate_up)
    activated = (jax.nn.silu(gate_up[:, :FF]) * gate_up[:, FF:]).astype(BF16)
    result = hidden + forward_product(activated, w_down)
    return result, (inputs, normed, projected, joined, hidden, normed_two, gate_up, activated)


def layer_backward(grad_out, saved, weights, tables):
    gains, w_in, w_out, w_gate_up, w_down = weights
    inputs, normed, projected, joined, hidden, normed_two, gate_up, activated = saved
    blocks = inputs.shape[0] // T
    grad_ffn = grad_out.astype(BF16)
    grad_act = back_product(grad_ffn, w_down)
    gate, up = gate_up[:, :FF], gate_up[:, FF:]
    sig = jax.nn.sigmoid(gate)
    grad_gate = (grad_act * up * (sig * (1.0 + gate * (1.0 - sig)))).astype(BF16)
    grad_up = (grad_act * (gate * sig)).astype(BF16)
    grad_gate_up = jnp.concatenate([grad_gate, grad_up], 1)
    grad_hidden, grad_gain_two = rms_back(hidden, gains[1], back_product(grad_gate_up, w_gate_up))
    grad_hidden = grad_out + grad_hidden
    grad_branch = grad_hidden.astype(BF16)
    grad_joined = back_product(grad_branch, w_out)
    grad_proj, grad_conv, grad_head, grad_skip = mix_backward(
        projected.reshape(blocks, T, PAD), grad_joined.reshape(blocks, T, UW), tables
    )
    grad_proj = grad_proj.reshape(blocks * T, PAD)
    grad_input, grad_gain_one = rms_back(inputs, gains[0], back_product(grad_proj, w_in))
    grad_input = grad_hidden + grad_input
    pairs = (
        (normed, grad_proj),
        (joined, grad_branch),
        (normed_two, grad_gate_up),
        (activated, grad_ffn),
    )
    return grad_input, pairs, (grad_gain_one, grad_gain_two, grad_conv, grad_head, grad_skip)


def across(array, by):
    return lax.ppermute(array, "section", [(0, 1)] if by > 0 else [(1, 0)])


def gather_weights(norm_gains, w_in, w_out, w_gate_up, w_down):
    filler = jnp.zeros((w_in.shape[0], PAD - PIN - 2), BF16)
    joined = jnp.concatenate([w_in, norm_gains, filler], 1)
    w_in_all, w_out_all, w_gate_up_all, w_down_all = [
        lax.all_gather(part, "shard", axis=0, tiled=True)
        for part in (joined, w_out, w_gate_up, w_down)
    ]
    gains = w_in_all[:, PIN : PIN + 2].astype(F32).T
    return gains, w_in_all, w_out_all, w_gate_up_all, w_down_all


def body(
    tokens,
    segment_ids,
    cotangent,
    norm_gains,
    w_in,
    conv_params,
    head_params,
    w_out,
    w_gate_up,
    w_down,
):
    section = lax.axis_index("section")
    blocks, _, width = tokens.shape
    rows = blocks * T
    weights = gather_weights(norm_gains[0], w_in[0], w_out[0], w_gate_up[0], w_down[0])
    conv_all = lax.all_gather(conv_params[0], "shard", axis=0, tiled=True)
    tables = mixer_tables(segment_ids[:, 0], conv_all.astype(F32), head_params[0].astype(F32))

    own = tokens.reshape(rows, width)
    first, _ = layer_forward(own.astype(F32), weights, tables)
    received = across(first.astype(BF16), 1)
    inputs = jnp.where(section == 0, own, received).astype(F32)
    result, saved = layer_forward(inputs, weights, tables)

    top = cotangent.reshape(rows, width)
    first_grad, _, _ = layer_backward(top.astype(F32), saved, weights, tables)
    coming = across(first_grad.astype(BF16), -1)
    grad_out = jnp.where(section == 1, top, coming).astype(F32)
    grad_input, pairs, smalls = layer_backward(grad_out, saved, weights, tables)

    grad_gain_one, grad_gain_two, grad_conv, grad_head, grad_skip = smalls
    sums = [outer_sum(left, right) for left, right in pairs]
    shards = lax.axis_size("shard")
    gains = jnp.stack([grad_gain_one, grad_gain_two], 1)
    conv = jnp.sum(grad_conv, 0)[: CONV + 1].T.reshape(shards, -1)
    conv = jnp.pad(conv, ((0, 0), (0, 640 - conv.shape[1]))).reshape(shards * 64, 10)
    head = jnp.sum(grad_head, 0)[:2, :MHEADS]
    skip = jnp.sum(jnp.sum(grad_skip, 0)[0].reshape(MHEADS, HEAD_WIDTH), 1)
    head = jnp.concatenate([head, skip[None]], 0).T.reshape(-1)
    head = jnp.pad(head, (0, 128 - head.shape[0])).reshape(64, 2)
    head = jnp.broadcast_to(head[None], (shards, 64, 2)).reshape(shards * 64, 2)
    extra = jnp.concatenate([gains, conv, head], 1).astype(BF16)
    sums[0] = lax.dynamic_update_slice(sums[0], extra, (0, PIN))
    out_in, out_out, out_gu, out_dn = scatter_sums(
        [g.reshape(2, 4, 2, g.shape[0] // 16, g.shape[1]) for g in sums]
    )
    out_gains = out_in[:, PIN : PIN + 2]
    out_conv = out_in[:, PIN + 2 : PIN + 12].reshape(-1)[: 112 * (CONV + 1)]
    out_head = out_in[:, PIN + 12 : PIN + 14].reshape(-1)[: MHEADS * 3]
    return (
        result.astype(BF16).reshape(1, blocks, T, width),
        grad_input.reshape(1, blocks, T, width),
        out_gains[None],
        out_in[None, :, :PIN],
        out_conv.reshape(1, 112, CONV + 1),
        out_head.reshape(1, MHEADS, 3),
        out_out[None],
        out_gu[None],
        out_dn[None],
    )


def solution(mesh):
    in_specs = (
        P(None, ("shard", "rep"), None),
        P(None, ("shard", "rep"), None),
        P(None, ("shard", "rep"), None),
        P("section", "shard", None),
        P("section", "shard", None),
        P("section", "shard", None),
        P("section", None, None),
        P("section", "shard", None),
        P("section", "shard", None),
        P("section", "shard", None),
    )
    out_specs = (
        P("section", None, ("shard", "rep"), None),
        P("section", None, ("shard", "rep"), None),
        P("section", "shard", None),
        P("section", "shard", None),
        P("section", "shard", None),
        P("section", None, None),
        P("section", "shard", None),
        P("section", "shard", None),
        P("section", "shard", None),
    )
    return jax.shard_map(body, mesh=mesh, in_specs=in_specs, out_specs=out_specs, check_vma=False)
```

time: 1100 us -> 494 us (0.45)
  waiting for transfers between devices: 456 us -> 162 us
  local copies, waits for them, and re-layouts: 201 us -> 20.7 us
  Pallas kernels: 0 us -> 154 us
  matrix products: 235 us -> 90.6 us
  other arithmetic: 122 us -> 7.5 us
  starting transfers between devices: 19 us -> 6.09 us
    reduce_scatter x3 -> x0, waiting for transfers between devices: 205 us -> none  [the longest x1 75.9 us: body(): lax.psum_scatter(bundle[4].astype(jnp.bfloat16), 'shard', scatter_dimensi...]
    pallas_call x0 -> x5, Pallas kernels: none -> 154 us  [the longest x1 111 us: scatter_sums(): pl.pallas_call(scatter_kernel, in_specs=[pl.BlockSpec(memory_space=pl.ANY...]
    dot_general x57 -> x8, matrix products: 146 us -> 34.6 us  [forward_product(): return jnp.dot(left, weight, preferred_element_type=F32)]
    unnamed x669 -> x52, local copies, waits for them, and re-layouts: 88 us -> 5.52 us
    unnamed x12 -> x4, waiting for transfers between devices: 77.4 us -> 1.92 us
    psum x1 -> x0, waiting for transfers between devices: 53.6 us -> none  [body(): lax.psum(owned[1].astype(jnp.bfloat16), 'rep').astype(jnp.float32)]
    slice x65 -> x7, local copies, waits for them, and re-layouts: 45.1 us -> 3.7 us  [the longest x2 1.47 us: body(): out_gains = out_in[:, PIN:PIN + 2]]
    reduce_sum x22 -> x4, other arithmetic: 30.8 us -> 0.15 us  [the longest x2 0.13 us: body(): skip = jnp.sum(jnp.sum(grad_skip, 0)[0].reshape(MHEADS, HEAD_WIDTH), 1)]
  transfers between devices with their start and end apart: 15 -> 6, of which waited for: 12 -> 6; matrix products, arithmetic and copies ran while one was open for 14% -> 4% of each run, Pallas kernels for 0% -> 1%
where the time goes in v1:
time: 494 us; the launch traced here: 484 us
  waiting for transfers between devices  162 us (33%)
  Pallas kernels  154 us (31%)
  matrix products  90.6 us (18%)
  blocking collectives  28.6 us (6%)
  local copies, waits for them, and re-layouts  20.7 us (4%)
  between operations  14.7 us (3%)
  other arithmetic  7.5 us (2%)
  starting transfers between devices  6.09 us (1%)
    all_gather x4, waiting for transfers between devices, gather_weights(): lax.all_gather(part, 'shard', axis=0, tiled=True)  137 us
    pallas_call x1, Pallas kernels, scatter_sums(): pl.pallas_call(scatter_kernel, in_specs=[pl.BlockSpec(memory_space=pl.ANY...  111 us
    dot_general x8, matrix products, back_product(): lax.dot_general(grad_rows, weight, (((1,), (1,)), ((), ())), preferred_el...  35.4 us
    dot_general x8, matrix products, forward_product(): return jnp.dot(left, weight, preferred_element_type=F32)  34.6 us
    pallas_call x2, Pallas kernels, mix_backward(): pl.pallas_call(mix_backward_kernel, grid=(blocks,), in_specs=[per_block((...  31.4 us
    all_gather x1, blocking collectives, body(): conv_all = lax.all_gather(conv_params[0], 'shard', axis=0, tiled=True)  28.6 us
    ppermute x2, waiting for transfers between devices, across(): return lax.ppermute(array, 'section', [(0, 1)] if by > 0 else [(1, 0)])  22.9 us
    dot_general x4, matrix products, outer_sum(): lax.dot_general(left, right, (((0,), (0,)), ((), ())), preferred_element_...  20.6 us
  transfers between devices with their start and end apart: 6, of which 6 were waited for; matrix products, arithmetic and copies ran while one was open for 4% of the time, Pallas kernels for 1%

profile of v1, /device:TPU:1, one launch (start us, length us, event | category | flops | bytes accessed | tf_op | source)
XLA Modules:
  0.0 484.2 jit_solution(14061970011970874226)
XLA Ops:
  14.3 28.6 %all-gather = bf16[1,1792,5]{2,0,1:T(2,128)(2,1)S(1)} all-gather(bf16[1,112,5]{2,0,1:T(2,128)(2,1)S(1)} %copy.43), channel_id=2, replica_groups=mesh['section'=2,'shard'=16,'rep'=4] {'shard'}, dimensions={1}, use_global_device_ids=true | all-gather | bytes 19040 | tf_op jit(solution)/shard_map/all_gather | solution.py:638
  43.9 25.8 %all-gather.9.cloned.1.call-done = bf16[1024,4224]{1,0:T(8,128)(2,1)} async-done(((bf16[64,4224]{1,0:T(8,128)(2,1)}), bf16[1024,4224]{1,0:T(8,128)(2,1)}) %all-gather.9.cloned.1.call-update) | async-done | bytes 8650768 | tf_op jit(solution)/shard_map/all_gather | solution.py:615
  71.3 5.7 %fusion.p_ref = f32[2,112,4224]{2,1,0:T(8,128)S(1)} fusion(bf16[1024,4224]{1,0:T(8,128)(2,1)} %all-gather.9.cloned.1.call-done, bf16[2,112,1024]{2,1,0:T(8,128)(2,1)S(1)} %copy-done.9, f32[1024]{0:T(1024)S(1)} %get-tuple-element.68, f32[2,112]{1,0:T(2,128)S(1)} %add_rsqrt_fusion.3), kind=kOutput, calls=%fused_computation.1 | convolution fusion | flops 1938685952 | bytes 12899200 | tf_op jit(solution)/shard_map/dot_general | solution.py:548
  77.1 5.9 %mix_forward.2 = bf16[2,112,2048]{2,1,0:T(8,128)(2,1)S(1)} custom-call(f32[2,112,4224]{2,1,0:T(8,128)S(1)} %fusion.p_ref, f32[2,112,128]{2,1,0:T(8,128)S(1)} %broadcast_in_dim.29.segc_ref, f32[2,8,112]{2,1,0:T(8,128)S(1)} %broadcast_in_dim.30.segr_ref, f32[8,1792]{1,0:T(8,128)S(1)} %pad_convert_fusion.conv_ref, f32[8,128]{1,0:T(8,128)S(1)} %pad.21.head_ref, ...), custom_call_target="tpu_custom_call" | custom-call | tf_op jit(solution)/shard_map/mix_forward/pallas_call | solution.py:247
  83.0 28.0 %all-gather.11.cloned.1.call-done = bf16[1,2048,1024]{2,1,0:T(8,128)(2,1)} async-done(((bf16[1,128,1024]{2,1,0:T(8,128)(2,1)}), bf16[1,2048,1024]{2,1,0:T(8,128)(2,1)}) %all-gather.11.cloned.1.call-update) | async-done | bytes 4194320 | tf_op jit(solution)/shard_map/all_gather | solution.py:615
  114.5 50.2 %all-gather.13.cloned.1.call-done = bf16[1,1024,4096]{2,1,0:T(8,128)(2,1)} async-done(((bf16[1,64,4096]{2,1,0:T(8,128)(2,1)}), bf16[1,1024,4096]{2,1,0:T(8,128)(2,1)}) %all-gather.13.cloned.1.call-update) | async-done | bytes 8388624 | tf_op jit(solution)/shard_map/all_gather | solution.py:615
  164.7 7.3 %fusion.8 = f32[224,4096]{1,0:T(8,128)} fusion(bf16[1,1024,4096]{2,1,0:T(8,128)(2,1)} %all-gather.13.cloned.1.call-done, f32[224,1024]{1,0:T(8,128)S(1)} %get-tuple-element.79, f32[1024]{0:T(1024)S(1)} %get-tuple-element.67, f32[224]{0:T(256)S(1)} %add_rsqrt_fusion.2), kind=kOutput, calls=%fused_computation.9 | convolution fusion | flops 1879736320 | bytes 12981120 | tf_op jit(solution)/shard_map/dot_general | solution.py:548
  172.0 32.7 %all-gather.15.cloned.1.call-done = bf16[1,2048,1024]{2,1,0:T(8,128)(2,1)} async-done(((bf16[1,128,1024]{2,1,0:T(8,128)(2,1)}), bf16[1,2048,1024]{2,1,0:T(8,128)(2,1)}) %all-gather.15.cloned.1.call-update) | async-done | bytes 4194320 | tf_op jit(solution)/shard_map/all_gather | solution.py:615
  204.7 4.5 fusion.56
  209.2 4.5 collective-permute-start
  213.7 9.6 %collective-permute-done = bf16[224,1024]{1,0:T(8,128)(2,1)S(1)} collective-permute-done((bf16[224,1024]{1,0:T(8,128)(2,1)S(1)}, bf16[224,1024]{1,0:T(8,128)(2,1)S(1)}, u32[]{:S(2)}, u32[]{:S(2)}) %collective-permute-start) | collective-permute-done | bytes 458784 | tf_op jit(solution)/shard_map/ppermute | solution.py:608
  223.6 6.0 %fusion.85 = f32[224,4224]{1,0:T(8,128)S(1)} fusion(bf16[1024,4224]{1,0:T(8,128)(2,1)} %all-gather.9.cloned.1.call-done, bf16[224,1024]{1,0:T(8,128)(2,1)S(1)} %get-tuple-element.70, f32[1024]{0:T(1024)S(1)} %get-tuple-element.68, f32[224]{0:T(256)S(1)} %add_rsqrt_fusion.1), kind=kOutput, calls=%fused_computation.101 | convolution fusion | flops 1938685952 | bytes 12899200 | tf_op jit(solution)/shard_map/dot_general | solution.py:548
  229.6 6.1 %mix_forward.3 = bf16[2,112,2048]{2,1,0:T(8,128)(2,1)S(1)} custom-call(f32[2,112,4224]{2,1,0:T(8,128)S(1)} %bitcast.116, f32[2,112,128]{2,1,0:T(8,128)S(1)} %broadcast_in_dim.29.segc_ref, f32[2,8,112]{2,1,0:T(8,128)S(1)} %broadcast_in_dim.30.segr_ref, f32[8,1792]{1,0:T(8,128)S(1)} %pad_convert_fusion.conv_ref, f32[8,128]{1,0:T(8,128)S(1)} %pad.21.head_ref, ...), custom_call_target="tpu_custom_call" | custom-call | tf_op jit(solution)/shard_map/mix_forward/pallas_call | solution.py:247
  242.7 4.4 multiply_reduce_fusion.2
  251.2 15.9 %mix_backward.2 = (bf16[2,112,4224]{2,1,0:T(8,128)(2,1)S(1)}, f32[2,8,1792]{2,1,0:T(8,128)}, f32[2,8,128]{2,1,0:T(8,128)}, f32[2,8,1536]{2,1,0:T(8,128)}) custom-call(f32[2,112,4224]{2,1,0:T(8,128)S(1)} %bitcast.117, f32[2,112,2048]{2,1,0:T(8,128)S(1)} %bitcast.120, f32[2,112,128]{2,1,0:T(8,128)S(1)} %broadcast_in_dim.29.segc_ref, ...), custom_call_target="tpu_custom_call" | custom-call | tf_op jit(solution)/shard_map/mix_backward/pallas_call | solution.py:261
  272.5 13.3 %collective-permute-done.1 = bf16[224,1024]{1,0:T(8,128)(2,1)S(1)} collective-permute-done((bf16[224,1024]{1,0:T(8,128)(2,1)}, bf16[224,1024]{1,0:T(8,128)(2,1)S(1)}, u32[]{:S(2)}, u32[]{:S(2)}) %collective-permute-start.1) | collective-permute-done | bytes 458784 | tf_op jit(solution)/shard_map/ppermute | solution.py:608
  285.9 6.2 %multiply_convert_fusion.1 = (bf16[224,2048]{1,0:T(8,128)(2,1)S(1)}, bf16[224,2048]{1,0:T(8,128)(2,1)S(1)}, bf16[224,2048]{1,0:T(8,128)(2,1)}) fusion(f32[224,4096]{1,0:T(8,128)} %copy-done.11, bf16[224,1024]{1,0:T(8,128)(2,1)S(1)} %broadcast_select_fusion, bf16[1,2048,1024]{2,1,0:T(8,128)(2,1)} %all-gather.15.cloned.1.call-done), kind=kOutput, calls=%fused_computation.37 | convolution fusion | flops 946405376 | bytes 11075584 | tf_op jit(solution)/shard_map/dot_general | solution.py:552
  292.1 5.7 %convolution_convert_fusion.1 = bf16[1024,4096]{1,0:T(8,128)(2,1)} fusion(bf16[224,2048]{1,0:T(8,128)(2,1)S(1)} %get-tuple-element.72, bf16[224,2048]{1,0:T(8,128)(2,1)S(1)} %get-tuple-element.71, f32[224,1024]{1,0:T(8,128)S(1)} %get-tuple-element.81, f32[224]{0:T(256)S(1)} %add_rsqrt_fusion, f32[1024]{0:T(1024)S(1)} %get-tuple-element.67), kind=kOutput, calls=%fused_computation.11 | convolution fusion | flops 1887600640 | bytes 11146112 | tf_op jit(solution)/shard_map/dot_general | solution.py:558
  297.8 6.3 %multiply_reduce_fusion = (bf16[1024]{0:T(1024)(128)(2,1)S(1)}, f32[224]{0:T(256)S(1)}, f32[224,1024]{1,0:T(8,128)S(1)}) fusion(f32[224,1024]{1,0:T(8,128)S(1)} %get-tuple-element.81, f32[224]{0:T(256)S(1)} %add_rsqrt_fusion, f32[1024]{0:T(1024)S(1)} %get-tuple-element.67, bf16[1,1024,4096]{2,1,0:T(8,128)(2,1)} %all-gather.13.cloned.1.call-done, ...), kind=kOutput, calls=%fused_computation.78 | convolution fusion | flops 1884093184 | bytes 12066560 | tf_op jit(solution)/shard_map/dot_general | solution.py:552
  309.8 15.4 %mix_backward.3 = (bf16[2,112,4224]{2,1,0:T(8,128)(2,1)S(1)}, f32[2,8,1792]{2,1,0:T(8,128)S(1)}, f32[2,8,128]{2,1,0:T(8,128)S(1)}, f32[2,8,1536]{2,1,0:T(8,128)S(1)}) custom-call(f32[2,112,4224]{2,1,0:T(8,128)S(1)} %bitcast.118, f32[2,112,2048]{2,1,0:T(8,128)S(1)} %bitcast.119, f32[2,112,128]{2,1,0:T(8,128)S(1)} %broadcast_in_dim.29.segc_ref, ...), custom_call_target="tpu_custom_call" | custom-call | tf_op jit(solution)/shard_map/mix_backward/pallas_call | solution.py:261
  325.9 7.1 %convolution_convert_fusion = bf16[1024,4224]{1,0:T(8,128)(2,1)} fusion(bf16[224,4224]{1,0:T(8,128)(2,1)S(1)} %bitcast.123, bf16[224,1024]{1,0:T(8,128)(2,1)} %copy-done.6, f32[1024]{0:T(1024)S(1)} %get-tuple-element.68, f32[224]{0:T(256)S(1)} %add_rsqrt_fusion.1), kind=kOutput, calls=%fused_computation | convolution fusion | flops 1943011328 | bytes 11006848 | tf_op jit(solution)/shard_map/dot_general | solution.py:558
  333.0 7.2 %fusion.72 = (bf16[1024]{0:T(1024)(128)(2,1)S(1)}, f32[224]{0:T(256)S(1)}, f32[224,1024]{1,0:T(8,128)}) fusion(bf16[224,1024]{1,0:T(8,128)(2,1)S(1)} %copy-done.7, f32[224]{0:T(256)S(1)} %add_rsqrt_fusion.1, f32[1024]{0:T(1024)S(1)} %get-tuple-element.68, bf16[224,4224]{1,0:T(8,128)(2,1)S(1)} %bitcast.124, bf16[1024,4224]{1,0:T(8,128)(2,1)} %all-gather.9.cloned.1.call-done), kind=kOutput, calls=%fused_computation.76 | convolution fusion | flops 1939372800 | bytes 11927296 | tf_op jit(solution)/shard_map/dot_general | solution.py:552
  341.8 4.6 convolution_convert_fusion.2
  350.1 111.1 %scatter_sums.1 = (f32[64,4224]{1,0:T(8,128)}, f32[128,1024]{1,0:T(8,128)}, f32[64,4096]{1,0:T(8,128)}, f32[128,1024]{1,0:T(8,128)}) custom-call(bf16[2,4,2,64,4224]{4,3,2,1,0:T(8,128)(2,1)} %bitcast.131, bf16[2,4,2,128,1024]{4,3,2,1,0:T(8,128)(2,1)} %bitcast.133, bf16[2,4,2,64,4096]{4,3,2,1,0:T(8,128)(2,1)} %bitcast.132, bf16[2,4,2,128,1024]{4,3,2,1,0:T(8,128)(2,1)} %bitcast.134), custom_call_target="tpu_custom_call" | custom-call | tf_op jit(solution)/shard_map/scatter_sums/pallas_call | solution.py:510
  (132 shorter events, 57.3 us)
Async XLA Ops:
  7.2 36.5 %copy-start.9 = (bf16[2,112,1024]{2,1,0:T(8,128)(2,1)S(1)}, bf16[2,112,1024]{2,1,0:T(8,128)(2,1)}, u32[]{:S(2)}) copy-start(bf16[2,112,1024]{2,1,0:T(8,128)(2,1)} %param.10) | copy-start | bytes 1376260
  7.2 62.5 %all-gather.9.cloned.1.call-start = ((), (), s32[]{:S(2)}) async-start(), calls=%async_computation | async-start | bytes 9191424 | tf_op jit(solution)/shard_map/all_gather | solution.py:615
  9.9 101.1 %all-gather.11.cloned.1.call-start = ((), (), s32[]{:S(2)}) async-start(), calls=%async_computation.1 | async-start | bytes 4456448 | tf_op jit(solution)/shard_map/all_gather | solution.py:615
  10.7 154.1 %all-gather.13.cloned.1.call-start = ((), (), s32[]{:S(2)}) async-start(), calls=%async_computation.2 | async-start | bytes 8912896 | tf_op jit(solution)/shard_map/all_gather | solution.py:615
  11.4 193.3 %all-gather.15.cloned.1.call-start = ((), (), s32[]{:S(2)}) async-start(), calls=%async_computation.3 | async-start | bytes 4456448 | tf_op jit(solution)/shard_map/all_gather | solution.py:615
  209.2 14.1 %collective-permute-start = (bf16[224,1024]{1,0:T(8,128)(2,1)S(1)}, bf16[224,1024]{1,0:T(8,128)(2,1)S(1)}, u32[]{:S(2)}, u32[]{:S(2)}) collective-permute-start(bf16[224,1024]{1,0:T(8,128)(2,1)S(1)} %fusion.56), channel_id=1, source_target_pairs={{0,64},{1,65},{2,66},{3,67},{4,68},{5,69},{6,70},{7,71},{8,72},{9,... | collective-permute-start | bytes 1376264 | tf_op jit(solution)/shard_map/ppermute | solution.py:608
  223.3 13.7 %slice-start = ((s8[8388608]{0:T(1024)(128)(4,1)}), s8[4194304]{0:T(1024)(128)(4,1)S(1)}, s32[]{:S(2)}) async-start(s8[8388608]{0:T(1024)(128)(4,1)} %bitcast.127), calls=%async_computation.4 | async-start | bytes 8388608
  223.5 46.4 %copy-start.6 = (bf16[224,1024]{1,0:T(8,128)(2,1)}, bf16[224,1024]{1,0:T(8,128)(2,1)S(1)}, u32[]{:S(2)}) copy-start(bf16[224,1024]{1,0:T(8,128)(2,1)S(1)} %get-tuple-element.70) | copy-start | bytes 1376260
  223.6 13.5 %slice-start.1 = ((s8[8388608]{0:T(1024)(128)(4,1)}), s8[4194304]{0:T(1024)(128)(4,1)S(1)}, s32[]{:S(2)}) async-start(s8[8388608]{0:T(1024)(128)(4,1)} %bitcast.127), calls=%async_computation.5 | async-start | bytes 8388608
  229.6 21.6 %copy-start = (f32[224,4224]{1,0:T(8,128)}, f32[224,4224]{1,0:T(8,128)S(1)}, u32[]{:S(2)}) copy-start(f32[224,4224]{1,0:T(8,128)S(1)} %fusion.85) | copy-start | bytes 11354116
  229.6 6.2 %copy-start.2 = (bf16[1,2048,1024]{2,1,0:T(8,128)(2,1)S(1)}, bf16[1,2048,1024]{2,1,0:T(8,128)(2,1)}, u32[]{:S(2)}) copy-start(bf16[1,2048,1024]{2,1,0:T(8,128)(2,1)} %all-gather.11.cloned.1.call-done) | copy-start | bytes 12582916
  239.3 3.4 copy-start.11
  242.7 24.5 %slice-start.2 = ((s8[8650752]{0:T(1024)(128)(4,1)}), s8[4194304]{0:T(1024)(128)(4,1)S(1)}, s32[]{:S(2)}) async-start(s8[8650752]{0:T(1024)(128)(4,1)} %bitcast.129), calls=%async_computation.6 | async-start | bytes 8388608
  242.7 24.5 %slice-start.3 = ((s8[8650752]{0:T(1024)(128)(4,1)}), s8[262144]{0:T(1024)(128)(4,1)S(1)}, s32[]{:S(2)}) async-start(s8[8650752]{0:T(1024)(128)(4,1)} %bitcast.129), calls=%async_computation.7 | async-start | bytes 524288
  247.4 19.7 %slice-start.4 = ((s8[8650752]{0:T(1024)(128)(4,1)}), s8[4194304]{0:T(1024)(128)(4,1)S(1)}, s32[]{:S(2)}) async-start(s8[8650752]{0:T(1024)(128)(4,1)} %bitcast.129), calls=%async_computation.8 | async-start | bytes 8388608
  271.0 14.8 %collective-permute-start.1 = (bf16[224,1024]{1,0:T(8,128)(2,1)}, bf16[224,1024]{1,0:T(8,128)(2,1)S(1)}, u32[]{:S(2)}, u32[]{:S(2)}) collective-permute-start(bf16[224,1024]{1,0:T(8,128)(2,1)} %fusion.67), channel_id=1, source_target_pairs={{64,0},{65,1},{66,2},{67,3},{68,4},{69,5},{70,6},{71,7},{72,8},{73... | collective-permute-start | bytes 1376264 | tf_op jit(solution)/shard_map/ppermute | solution.py:608
  285.9 18.2 %copy-start.10 = (bf16[224,1024]{1,0:T(8,128)(2,1)}, bf16[224,1024]{1,0:T(8,128)(2,1)S(1)}, u32[]{:S(2)}) copy-start(bf16[224,1024]{1,0:T(8,128)(2,1)S(1)} %broadcast_select_fusion) | copy-start | bytes 1376260
  325.9 7.1 %copy-start.7 = (bf16[224,1024]{1,0:T(8,128)(2,1)S(1)}, bf16[224,1024]{1,0:T(8,128)(2,1)}, u32[]{:S(2)}) copy-start(bf16[224,1024]{1,0:T(8,128)(2,1)} %copy-done.6) | copy-start | bytes 1376260
  350.1 118.0 %copy-start.5 = (f32[224,1024]{1,0:T(8,128)S(1)}, f32[224,1024]{1,0:T(8,128)}, u32[]{:S(2)}) copy-start(f32[224,1024]{1,0:T(8,128)} %copy-done.4) | copy-start | bytes 2752516
  350.1 118.0 %copy-start.8 = (bf16[224,1024]{1,0:T(8,128)(2,1)S(1)}, bf16[224,1024]{1,0:T(8,128)(2,1)}, u32[]{:S(2)}) copy-start(bf16[224,1024]{1,0:T(8,128)(2,1)} %copy-done.6) | copy-start | bytes 1376260
  461.2 9.3 %copy-start.12 = (bf16[224,2048]{1,0:T(8,128)(2,1)S(1)}, bf16[224,2048]{1,0:T(8,128)(2,1)}, u32[]{:S(2)}) copy-start(bf16[224,2048]{1,0:T(8,128)(2,1)} %get-tuple-element.75) | copy-start | bytes 2752516
  470.5 4.2 copy-start.16
  470.5 5.0 %copy-start.14 = (f32[64,4096]{1,0:T(8,128)S(1)}, f32[64,4096]{1,0:T(8,128)}, u32[]{:S(2)}) copy-start(f32[64,4096]{1,0:T(8,128)} %get-tuple-element.25) | copy-start | bytes 3145732
  470.5 6.0 %copy-start.15 = (f32[128,1024]{1,0:T(8,128)S(1)}, f32[128,1024]{1,0:T(8,128)}, u32[]{:S(2)}) copy-start(f32[128,1024]{1,0:T(8,128)} %get-tuple-element.26) | copy-start | bytes 1572868
  (5 other events, 13.3 us)
Sparse Core Ops, SparseCore 0:
  10.3 59.3 all-gather.8
  71.4 39.6 all-gather.10
  112.8 51.9 all-gather.12
  166.3 38.3 all-gather.14
